TPU v7x, 32 devices: a whole 2x2x4 slice. The times are simulated.
32 devices in a mesh: groups: 2 (over y), chan: 4 (over z), tm: 2 (over x), band: 2 (over core).
Axes of the slice: x: 2, y: 2, z: 4, core: 2. Of those that a mesh axis runs over, the one named last changes fastest.
Arguments:
- recording: float32 [1024, 2048], P(('groups', 'chan'), 'tm'), parts along dimension 0, may hold values from -460 to 460
- tau_index: int32 [1024], P(('groups', 'chan')), parts along dimension 0, may hold values from 0 to 7
- pair_offset: int32 [4, 4], replicated, may hold values from -1 to 3, as said below
Outputs:
- correlations: float32 [8, 4, 3, 128, 128], P(('groups', 'chan'), None, None, ('tm', 'band')), parts along dimension 0
There are 2 independent parts, one for each index of `groups`. A program takes and returns all parts, laid end to end along the dimension named above; an argument that names none is the same for every part. Nothing has to cross between parts.
Inputs may be any that keep to these rules, and one draw needn't show every extreme that they name: pair_offset[i, q] is an offset of 1 to 3 blocks for q below the row's partner count, and -1 from there on; every row has 1 to 4 partners.
All inputs are finite; a program needn't handle non-finite values.
Results may differ from a plain program's by a relative error of at most 0.006.
Values may be sent and summed in bfloat16 or wider, within the bound.
A program may use at most 64 MiB of HBM per device.

v0:
```python
import math
import jax
import jax.numpy as jnp
from jax import lax
from jax.sharding import PartitionSpec as P

BLK = 128
HALO_CH = 64
HALO_T = 256
LAGS = 3
QMAX = 4


def from_behind(block, axis, distance):
    devices = range(lax.axis_size(axis))
    route = [(i - distance, i) for i in devices if i - distance in devices]
    return lax.ppermute(block, axis, route)


def padded_2(block, sides, width):
    for axis, dim in sides:
        count = lax.axis_size(axis)
        forward = [(i, i + 1) for i in range(count - 1)]
        backward = [(target, source) for source, target in forward]
        low = lax.ppermute(
            lax.slice_in_dim(block, block.shape[dim] - width, None, axis=dim), axis, forward
        )
        high = lax.ppermute(lax.slice_in_dim(block, 0, width, axis=dim), axis, backward)
        block = jnp.concatenate([low, block, high], axis=dim)
    return block


def slide_total(padded, reach, size, axis):
    zero_shape = list(padded.shape)
    zero_shape[axis] = 1
    running = jnp.concatenate(
        [jnp.zeros(zero_shape, jnp.float32), jnp.cumsum(padded, axis=axis)], axis=axis
    )
    upper = lax.slice_in_dim(running, 2 * reach + 1, 2 * reach + 1 + size, axis=axis)
    lower = lax.slice_in_dim(running, 0, size, axis=axis)
    return upper - lower


def spatial_filter(padded, center, counted):
    total = slide_total(padded, HALO_CH, center.shape[0], 0)
    return center - total / counted[:, None]


def amplitude_norm(padded, center):
    total = slide_total(jnp.abs(padded), HALO_T, center.shape[1], 1)
    return center / (total / (2.0 * HALO_T + 1.0) + 1e-06)


def shards(recording, tau_index, pair_offset):
    channels, samples = recording.shape
    chan_count = lax.axis_size("chan")
    time_count = lax.axis_size("tm")
    band_count = lax.axis_size("band")
    chan_pos = lax.axis_index("chan")
    time_pos = lax.axis_index("tm")
    band_pos = lax.axis_index("band")
    all_channels = channels * chan_count
    all_samples = samples * time_count
    kept_bins = all_samples // 4
    first_bin = kept_bins // 4
    band_bins = kept_bins // band_count
    device_bins = band_bins // time_count
    decay = jnp.exp(-1.0 / (2.0 * 2.0 ** (tau_index.astype(jnp.float32) / 2.0)))[:, None]
    rows_global = chan_pos * channels + jnp.arange(channels)
    counted = (
        jnp.minimum(rows_global, HALO_CH) + jnp.minimum(all_channels - 1 - rows_global, HALO_CH) + 1
    ).astype(jnp.float32)
    previous = from_behind(recording[:, samples - 1 :], "tm", 1)
    deconv = recording - decay * jnp.concatenate([previous, recording[:, : samples - 1]], axis=1)
    deconv_wide = padded_2(deconv, (("chan", 0),), HALO_CH)
    filtered = spatial_filter(deconv_wide, deconv, counted)
    filtered_wide = padded_2(filtered, (("tm", 1),), HALO_T)
    normed = amplitude_norm(filtered_wide, filtered)
    time_global = time_pos * samples + jnp.arange(samples)
    sub_rows = math.gcd(device_bins * lax.axis_size("tm"), 128)
    pieces = device_bins * lax.axis_size("tm") // sub_rows

    def one_piece(piece_idx):
        bins_here = first_bin + band_pos * band_bins + piece_idx * sub_rows + jnp.arange(sub_rows)
        turns = bins_here[:, None] * time_global[None, :] % all_samples
        angle = 2.0 * jnp.pi / all_samples * turns.astype(jnp.float32)
        dims = (((1,), (1,)), ((), ()))
        real_part = lax.dot_general(
            jnp.cos(angle),
            normed,
            dims,
            precision=lax.Precision.HIGHEST,
            preferred_element_type=jnp.float32,
        )
        imag_part = -lax.dot_general(
            jnp.sin(angle),
            normed,
            dims,
            precision=lax.Precision.HIGHEST,
            preferred_element_type=jnp.float32,
        )
        return jnp.stack([real_part, imag_part], axis=1)

    stacked = lax.map(one_piece, jnp.arange(pieces))
    spectra = lax.psum_scatter(
        stacked.reshape(device_bins * lax.axis_size("tm"), 2, channels),
        "tm",
        scatter_dimension=0,
        tiled=True,
    )
    local_power = jnp.sum(spectra * spectra, axis=(0, 1))
    power = lax.psum(local_power, ("tm", "band"))
    factor = lax.rsqrt(power / kept_bins + 1e-06)
    white = (spectra * factor[None, None, :]).astype(jnp.bfloat16)
    bins_mine = first_bin + band_pos * band_bins + time_pos * device_bins + jnp.arange(device_bins)
    lagged = jnp.arange(LAGS) - LAGS // 2
    phase = (
        2.0
        * jnp.pi
        / all_samples
        * (bins_mine[:, None] * lagged[None, :] % all_samples).astype(jnp.float32)
    )
    cosine = jnp.cos(phase)[:, :, None]
    sine = jnp.sin(phase)[:, :, None]
    white_f = white.astype(jnp.float32)
    real_shift = white_f[:, 0, None, :] * cosine - white_f[:, 1, None, :] * sine
    imag_shift = white_f[:, 0, None, :] * sine + white_f[:, 1, None, :] * cosine
    shifted = jnp.stack([real_shift, imag_shift], axis=1).astype(jnp.bfloat16)
    own_blocks = channels // BLK
    all_blocks = all_channels // BLK
    my_offsets = lax.dynamic_slice_in_dim(pair_offset, chan_pos * own_blocks, own_blocks, 0)
    left_blocks = [shifted.reshape(2 * device_bins, LAGS * BLK)]
    cc_scale = 1.0 / math.sqrt(kept_bins)
    initial = tuple(
        (jnp.zeros((LAGS * BLK, BLK), jnp.float32) for slot_all in range(own_blocks * QMAX))
    )
    piece = lax.all_gather(white, "chan", axis=2, tiled=True)
    width = piece.shape[2]
    updated = []
    for slot_idx in range(QMAX):
        offset = my_offsets[0, slot_idx]
        partner = (chan_pos * own_blocks + 0 + jnp.maximum(offset, 0)) % all_blocks
        local_col = partner * BLK
        present = (offset >= 0) & (local_col >= 0) & (local_col < width)
        clipped = jnp.clip(local_col, 0, width - BLK)
        right = lax.dynamic_slice_in_dim(piece, clipped, BLK, 2)
        right = right.reshape(2 * device_bins, BLK)

        def compute(previous_value, left=left_blocks[0], right=right):
            product = lax.dot_general(
                left, right, (((0,), (0,)), ((), ())), preferred_element_type=jnp.float32
            )
            return product * cc_scale

        def keep(previous_value):
            return previous_value

        updated.append(lax.cond(present, compute, keep, initial[slot_idx]))
    gathered = tuple(updated)
    stacked_cc = jnp.stack(gathered).reshape(own_blocks, QMAX, LAGS, BLK, BLK)
    return lax.psum_scatter(stacked_cc, ("tm", "band"), scatter_dimension=3, tiled=True)


def solution(mesh):
    return jax.shard_map(
        shards,
        mesh=mesh,
        in_specs=(P(("groups", "chan"), "tm"), P(("groups", "chan")), P()),
        out_specs=P(("groups", "chan"), None, None, ("tm", "band"), None),
        check_vma=False,
    )
```

profile of v0, /device:TPU:0, one launch (start us, length us, event | category | flops | bytes accessed | tf_op | source)
XLA Modules:
  0.0 122.5 jit_solution(3115787574492478725)
XLA Ops:
  6.5 0.9 slice.63
  7.5 4.8 %collective-permute-start = (f32[128,1]{1,0:T(8,128)S(1)}, f32[128,1]{1,0:T(8,128)S(1)}, u32[]{:S(2)}, u32[]{:S(2)}) collective-permute-start(f32[128,1]{1,0:T(8,128)S(1)} %slice.63), channel_id=1, source_target_pairs={{0,2},{1,3},{4,6},{5,7},{8,10},{9,11},{12,14},{13,15},{16,18},{17,... | collective-permute-start | bytes 1544 | tf_op jit(solution)/shard_map/ppermute | solution.py:17
  12.3 0.7 divide_exponential_fusion
  13.0 1.2 collective-permute-done
  14.2 1.4 %fusion.34 = f32[128,1024]{1,0:T(8,128)S(1)} fusion(f32[128,1024]{1,0:T(8,128)} %param.13, f32[128,1023]{1,0:T(8,128)} %bitcast.94, f32[128,1]{1,0:T(8,128)S(1)} %collective-permute-done, f32[128]{0:T(128)S(1)} %divide_exponential_fusion), kind=kLoop, calls=%fused_computation.55 | loop fusion | flops 393216 | bytes 1573376 | tf_op jit(solution)/shard_map/sub | solution.py:74
  15.7 3.5 %collective-permute-start.1 = (f32[64,1024]{1,0:T(8,128)S(1)}, f32[64,1024]{1,0:T(8,128)S(1)}, u32[]{:S(2)}, u32[]{:S(2)}) collective-permute-start(f32[64,1024]{1,0:T(8,128)S(1)} %get-tuple-element.262), channel_id=1, source_target_pairs={{0,4},{4,8},{8,12},{1,5},{5,9},{9,13},{2,6},{6,10},{10,14},{3,7},{... | collective-permute-start | bytes 786440 | tf_op jit(solution)/shard_map/ppermute | solution.py:25
  19.2 1.3 %collective-permute-start.2 = (f32[64,1024]{1,0:T(8,128)S(1)}, f32[64,1024]{1,0:T(8,128)S(1)}, u32[]{:S(2)}, u32[]{:S(2)}) collective-permute-start(f32[64,1024]{1,0:T(8,128)S(1)} %get-tuple-element.263), channel_id=1, source_target_pairs={{4,0},{8,4},{12,8},{5,1},{9,5},{13,9},{6,2},{10,6},{14,10},{7,3},{... | collective-permute-start | bytes 786440 | tf_op jit(solution)/shard_map/ppermute | solution.py:28
  20.5 3.4 %collective-permute-done.1 = f32[64,1024]{1,0:T(8,128)S(1)} collective-permute-done((f32[64,1024]{1,0:T(8,128)S(1)}, f32[64,1024]{1,0:T(8,128)S(1)}, u32[]{:S(2)}, u32[]{:S(2)}) %collective-permute-start.1) | collective-permute-done | bytes 262176 | tf_op jit(solution)/shard_map/ppermute | solution.py:25
  23.9 4.1 %collective-permute-done.2 = f32[64,1024]{1,0:T(8,128)S(1)} collective-permute-done((f32[64,1024]{1,0:T(8,128)S(1)}, f32[64,1024]{1,0:T(8,128)S(1)}, u32[]{:S(2)}, u32[]{:S(2)}) %collective-permute-start.2) | collective-permute-done | bytes 262176 | tf_op jit(solution)/shard_map/ppermute | solution.py:28
  28.1 0.8 fusion.25
  29.6 4.0 %collective-permute-start.3 = (f32[128,256]{1,0:T(8,128)S(1)}, f32[128,256]{1,0:T(8,128)S(1)}, u32[]{:S(2)}, u32[]{:S(2)}) collective-permute-start(f32[128,256]{1,0:T(8,128)S(1)} %get-tuple-element.260), channel_id=1, source_target_pairs={{0,2},{1,3},{4,6},{5,7},{8,10},{9,11},{12,14},{13,15},{16,18},{17,... | collective-permute-start | bytes 393224 | tf_op jit(solution)/shard_map/ppermute | solution.py:25
  33.6 1.3 %collective-permute-start.4 = (f32[128,256]{1,0:T(8,128)S(1)}, f32[128,256]{1,0:T(8,128)S(1)}, u32[]{:S(2)}, u32[]{:S(2)}) collective-permute-start(f32[128,256]{1,0:T(8,128)S(1)} %get-tuple-element.261), channel_id=1, source_target_pairs={{2,0},{3,1},{6,4},{7,5},{10,8},{11,9},{14,12},{15,13},{18,16},{19,... | collective-permute-start | bytes 393224 | tf_op jit(solution)/shard_map/ppermute | solution.py:28
  34.9 1.2 collective-permute-done.3
  36.0 4.4 %collective-permute-done.4 = f32[128,256]{1,0:T(8,128)S(1)} collective-permute-done((f32[128,256]{1,0:T(8,128)S(1)}, f32[128,256]{1,0:T(8,128)S(1)}, u32[]{:S(2)}, u32[]{:S(2)}) %collective-permute-start.4) | collective-permute-done | bytes 131104 | tf_op jit(solution)/shard_map/ppermute | solution.py:28
  42.1 13.2 %while.13 = (s32[]{:T(128)}, f32[2,128,2,128]{3,1,0,2:T(8,128)S(1)}, s32[2]{0:T(128)S(1)}, s32[]{:T(128)}, f32[128,1024]{1,0:T(8,128)S(1)}, /*index=5*/s32[]{:T(128)}, s32[]{:T(128)}, s32[1]{0:T(128)}) while((s32[]{:T(128)}, f32[2,128,2,128]{3,1,0,2:T(8,128)S(1)}, s32[2]{0:T(128)S(1)}, s32[]{:T(128)}, f32[128,1024]{1,0:T(8,128)S(1)}, ...), condition=%wide.region_5.6_spmd.clone, body=%wide.region_4.5_spmd.clone.sunk | while | flops 406373504 | bytes 1455749 | solution.py:104
  43.5 2.6 %convolution_bitcast_fusion.2 = f32[128,1,128]{2,0,1:T(8,128)S(1)} fusion(f32[128,1024]{1,0:T(8,128)S(1)} %get-tuple-element.331, s32[1024]{0:T(1024)S(1)} %iota_add_fusion.6, s32[128]{0:T(128)S(1)} %iota_add_fusion.7), kind=kOutput, calls=%fused_computation.15.clone.1 | convolution fusion | flops 203161600 | bytes 594432 | tf_op jit(solution)/shard_map/while/body/eval_jaxpr/dot_general | solution.py:88
  46.1 2.6 %fusion.64 = f32[128,1,128]{2,0,1:T(8,128)S(1)} fusion(f32[128,1024]{1,0:T(8,128)S(1)} %get-tuple-element.331, s32[1024]{0:T(1024)S(1)} %iota_add_fusion.6, s32[128]{0:T(128)S(1)} %iota_add_fusion.7), kind=kOutput, calls=%fused_computation.14.clone.1 | convolution fusion | flops 203177984 | bytes 594432 | tf_op jit(solution)/shard_map/while/body/eval_jaxpr/dot_general | solution.py:95
  50.1 2.6 %convolution_bitcast_fusion.2 = f32[128,1,128]{2,0,1:T(8,128)S(1)} fusion(f32[128,1024]{1,0:T(8,128)S(1)} %get-tuple-element.331, s32[1024]{0:T(1024)S(1)} %iota_add_fusion.6, s32[128]{0:T(128)S(1)} %iota_add_fusion.7), kind=kOutput, calls=%fused_computation.15.clone.1 | convolution fusion | flops 203161600 | bytes 594432 | tf_op jit(solution)/shard_map/while/body/eval_jaxpr/dot_general | solution.py:88
  52.7 2.6 %fusion.64 = f32[128,1,128]{2,0,1:T(8,128)S(1)} fusion(f32[128,1024]{1,0:T(8,128)S(1)} %get-tuple-element.331, s32[1024]{0:T(1024)S(1)} %iota_add_fusion.6, s32[128]{0:T(128)S(1)} %iota_add_fusion.7), kind=kOutput, calls=%fused_computation.14.clone.1 | convolution fusion | flops 203177984 | bytes 594432 | tf_op jit(solution)/shard_map/while/body/eval_jaxpr/dot_general | solution.py:95
  55.3 0.7 copy-done.1
  56.1 0.7 fusion.43
  62.3 4.9 %reduce-scatter.3.cloned.1.call-done = f32[128,2,128]{2,0,1:T(8,128)} async-done(((f32[256,2,128]{2,0,1:T(8,128)}), f32[128,2,128]{2,0,1:T(8,128)}) %reduce-scatter.3.cloned.1.call-update) | async-done | bytes 131088 | tf_op jit(solution)/shard_map/reduce_scatter | solution.py:105
  67.1 1.0 multiply_reduce_fusion
  68.1 5.8 %psum.7 = f32[128]{0:T(128)S(1)} all-reduce(f32[128]{0:T(128)S(1)} %multiply_reduce_fusion), channel_id=1, replica_groups=mesh['groups'=2,'chan'=4,'tm'=2,'band'=2] {'tm','band'}, use_global_device_ids=true, to_apply=%region_8.9 | all-reduce | flops 128 | bytes 1024 | tf_op jit(solution)/shard_map/psum | solution.py:112
  73.9 0.9 fusion.40
  75.4 13.0 %all_gather.3 = bf16[128,2,512]{2,0,1:T(8,128)(2,1)S(1)} all-gather(bf16[128,2,128]{2,0,1:T(8,128)(2,1)S(1)} %get-tuple-element.259), channel_id=1, replica_groups=mesh['groups'=2,'chan'=4,'tm'=2,'band'=2] {'chan'}, dimensions={2}, use_global_device_ids=true | all-gather | bytes 327680 | tf_op jit(solution)/shard_map/all_gather | solution.py:137
  88.4 0.8 conditional.4
  89.2 0.8 conditional.5
  90.0 0.8 conditional.6
  90.8 0.8 conditional.7
  91.6 1.0 pad_maximum_fusion.1
  92.6 23.1 %reduce-scatter.5.cloned.1.call-done = f32[1,4,3,32,128]{4,3,2,1,0:T(8,128)} async-done(((f32[1,4,3,128,128]{4,3,2,1,0:T(8,128)}), f32[1,4,3,32,128]{4,3,2,1,0:T(8,128)}) %reduce-scatter.5.cloned.1.call-update) | async-done | bytes 196624 | tf_op jit(solution)/shard_map/reduce_scatter | solution.py:161
  (64 shorter events, 7.8 us)
Async XLA Ops:
  6.5 28.3 %copy-start = (s32[4,4]{1,0:T(4,128)S(1)}, s32[4,4]{1,0:T(4,128)}, u32[]{:S(2)}) copy-start(s32[4,4]{1,0:T(4,128)} %param.15) | copy-start | bytes 196
  6.5 60.6 %reduce-scatter.3.cloned.1.call-start = ((), (), s32[]{:S(2)}) async-start(), calls=%async_computation.2 | async-start | bytes 393216 | tf_op jit(solution)/shard_map/reduce_scatter | solution.py:105
  7.5 6.7 %collective-permute-start = (f32[128,1]{1,0:T(8,128)S(1)}, f32[128,1]{1,0:T(8,128)S(1)}, u32[]{:S(2)}, u32[]{:S(2)}) collective-permute-start(f32[128,1]{1,0:T(8,128)S(1)} %slice.63), channel_id=1, source_target_pairs={{0,2},{1,3},{4,6},{5,7},{8,10},{9,11},{12,14},{13,15},{16,18},{17,... | collective-permute-start | bytes 1544 | tf_op jit(solution)/shard_map/ppermute | solution.py:17
  15.7 8.2 %collective-permute-start.1 = (f32[64,1024]{1,0:T(8,128)S(1)}, f32[64,1024]{1,0:T(8,128)S(1)}, u32[]{:S(2)}, u32[]{:S(2)}) collective-permute-start(f32[64,1024]{1,0:T(8,128)S(1)} %get-tuple-element.262), channel_id=1, source_target_pairs={{0,4},{4,8},{8,12},{1,5},{5,9},{9,13},{2,6},{6,10},{10,14},{3,7},{... | collective-permute-start | bytes 786440 | tf_op jit(solution)/shard_map/ppermute | solution.py:25
  19.2 8.8 %collective-permute-start.2 = (f32[64,1024]{1,0:T(8,128)S(1)}, f32[64,1024]{1,0:T(8,128)S(1)}, u32[]{:S(2)}, u32[]{:S(2)}) collective-permute-start(f32[64,1024]{1,0:T(8,128)S(1)} %get-tuple-element.263), channel_id=1, source_target_pairs={{4,0},{8,4},{12,8},{5,1},{9,5},{13,9},{6,2},{10,6},{14,10},{7,3},{... | collective-permute-start | bytes 786440 | tf_op jit(solution)/shard_map/ppermute | solution.py:28
  29.6 6.5 %collective-permute-start.3 = (f32[128,256]{1,0:T(8,128)S(1)}, f32[128,256]{1,0:T(8,128)S(1)}, u32[]{:S(2)}, u32[]{:S(2)}) collective-permute-start(f32[128,256]{1,0:T(8,128)S(1)} %get-tuple-element.260), channel_id=1, source_target_pairs={{0,2},{1,3},{4,6},{5,7},{8,10},{9,11},{12,14},{13,15},{16,18},{17,... | collective-permute-start | bytes 393224 | tf_op jit(solution)/shard_map/ppermute | solution.py:25
  33.6 6.9 %collective-permute-start.4 = (f32[128,256]{1,0:T(8,128)S(1)}, f32[128,256]{1,0:T(8,128)S(1)}, u32[]{:S(2)}, u32[]{:S(2)}) collective-permute-start(f32[128,256]{1,0:T(8,128)S(1)} %get-tuple-element.261), channel_id=1, source_target_pairs={{2,0},{3,1},{6,4},{7,5},{10,8},{11,9},{14,12},{15,13},{18,16},{19,... | collective-permute-start | bytes 393224 | tf_op jit(solution)/shard_map/ppermute | solution.py:28
  55.3 0.7 copy-start.1
  56.0 59.6 %reduce-scatter.5.cloned.1.call-start = ((), (), s32[]{:S(2)}) async-start(), calls=%async_computation.3 | async-start | bytes 983040 | tf_op jit(solution)/shard_map/reduce_scatter | solution.py:161
Sparse Core Ops, SparseCore 0:
  56.1 10.9 reduce-scatter.2
  92.7 22.9 reduce-scatter.4
where the time goes:
time: 123 us
  waiting for transfers between devices  42.2 us (34%)
  between operations  18.9 us (15%)
  blocking collectives  18.8 us (15%)
  starting transfers between devices  14.9 us (12%)
  matrix products  11.1 us (9%)
  other arithmetic  7.65 us (6%)
  local copies, waits for them, and re-layouts  7.28 us (6%)
  loops' own time  1.66 us (1%)
    reduce_scatter x1, waiting for transfers between devices, shards(): lax.psum_scatter(stacked_cc, ('tm', 'band'), scatter_dimension=3, tiled=T...  23.1 us
    all_gather x1, blocking collectives, shards(): piece = lax.all_gather(white, 'chan', axis=2, tiled=True)  13 us
    ppermute x2, waiting for transfers between devices, padded_2(): lax.ppermute(lax.slice_in_dim(block, 0, width, axis=dim), axis, backward)  8.49 us
    ppermute x2, starting transfers between devices, padded_2(): lax.ppermute(lax.slice_in_dim(block, block.shape[dim] - width, None, axis...  7.47 us
    psum x1, blocking collectives, shards(): power = lax.psum(local_power, ('tm', 'band'))  5.75 us
    dot_general x2, matrix products, one_piece(): lax.dot_general(jnp.sin(angle), normed, dims, precision=lax.Precision.HIG...  5.16 us
    dot_general x2, matrix products, one_piece(): lax.dot_general(jnp.cos(angle), normed, dims, precision=lax.Precision.HIG...  5.13 us
    reduce_scatter x1, waiting for transfers between devices, shards(): lax.psum_scatter(stacked.reshape(device_bins * lax.axis_size('tm'), 2, ch...  4.85 us
  transfers between devices with their start and end apart: 7, of which 7 were waited for; matrix products, arithmetic and copies ran while one was open for 1% of the time, Pallas kernels for 0%

commit v1 on v0

--- a/solution.py
+++ b/solution.py
@@ -134,7 +134,29 @@
     initial = tuple(
         (jnp.zeros((LAGS * BLK, BLK), jnp.float32) for slot_all in range(own_blocks * QMAX))
     )
-    piece = lax.all_gather(white, "chan", axis=2, tiled=True)
+    base_arr = lax.axis_index("chan")
+    local_part = lax.axis_size("chan")
+    k_now, local_now, heard = (local_part, base_arr, white.shape[2])
+    chunks = []
+    for no in range(k_now):
+        chunks.append((no, (no + 1) % k_now))
+    history = []
+    for no in range(k_now):
+        history.append((no, (no - 1) % k_now))
+    piece = jnp.zeros((*white.shape[:2], k_now * heard, *white.shape[3:]), white.dtype)
+    piece = lax.dynamic_update_slice_in_dim(piece, white, local_now * heard, axis=2)
+    tall = x_now = white
+    arr_now = k_now // 2
+    for jj in range(1, arr_now + 1):
+        tall = lax.ppermute(tall, axis_name="chan", perm=chunks)
+        piece = lax.dynamic_update_slice_in_dim(
+            piece, tall, (local_now - jj) % k_now * heard, axis=2
+        )
+        if jj < k_now - arr_now:
+            x_now = lax.ppermute(x_now, "chan", perm=history)
+            piece = lax.dynamic_update_slice_in_dim(
+                piece, x_now, (local_now + jj) % k_now * heard, axis=2
+            )
     width = piece.shape[2]
     updated = []
     for slot_idx in range(QMAX):

time: 123 us -> 119 us (0.967)
  blocking collectives: 18.8 us -> 5.75 us
  waiting for transfers between devices: 42.2 us -> 48.1 us
  starting transfers between devices: 14.9 us -> 18.8 us
    all_gather x1 -> x0, blocking collectives: 13 us -> none  [shards(): piece = lax.all_gather(white, 'chan', axis=2, tiled=True)]
    ppermute x0 -> x3, waiting for transfers between devices: none -> 7.84 us  [the longest x2 7.84 us: shards(): tall = lax.ppermute(tall, axis_name='chan', perm=chunks)]
    ppermute x0 -> x3, starting transfers between devices: none -> 3.88 us  [the longest x1 2.16 us: shards(): x_now = lax.ppermute(x_now, 'chan', perm=history)]
    reduce_scatter x1, waiting for transfers between devices: 23.1 us -> 21.2 us  [shards(): lax.psum_scatter(stacked_cc, ('tm', 'band'), scatter_dimension=3, tiled=T...]
  transfers between devices with their start and end apart: 7 -> 10, of which waited for: 7 -> 9; matrix products, arithmetic and copies ran while one was open for 1% -> 2% of each run, Pallas kernels for 0% -> 0%
where the time goes in v1:
time: 119 us
  waiting for transfers between devices  48.1 us (40%)
  between operations  18.9 us (16%)
  starting transfers between devices  18.8 us (16%)
  matrix products  11.2 us (9%)
  other arithmetic  7.65 us (6%)
  local copies, waits for them, and re-layouts  6.7 us (6%)
  blocking collectives  5.75 us (5%)
  loops' own time  1.51 us (1%)
    reduce_scatter x1, waiting for transfers between devices, shards(): lax.psum_scatter(stacked_cc, ('tm', 'band'), scatter_dimension=3, tiled=T...  21.2 us
    ppermute x2, waiting for transfers between devices, padded_2(): lax.ppermute(lax.slice_in_dim(block, 0, width, axis=dim), axis, backward)  8.49 us
    ppermute x2, waiting for transfers between devices, shards(): tall = lax.ppermute(tall, axis_name='chan', perm=chunks)  7.84 us
    ppermute x2, starting transfers between devices, padded_2(): lax.ppermute(lax.slice_in_dim(block, block.shape[dim] - width, None, axis...  7.47 us
    psum x1, blocking collectives, shards(): power = lax.psum(local_power, ('tm', 'band'))  5.75 us
    dot_general x2, matrix products, one_piece(): lax.dot_general(jnp.sin(angle), normed, dims, precision=lax.Precision.HIG...  5.16 us
    dot_general x2, matrix products, one_piece(): lax.dot_general(jnp.cos(angle), normed, dims, precision=lax.Precision.HIG...  5.14 us
    reduce_scatter x1, waiting for transfers between devices, shards(): lax.psum_scatter(stacked.reshape(device_bins * lax.axis_size('tm'), 2, ch...  4.9 us
  transfers between devices with their start and end apart: 10, of which 9 were waited for; matrix products, arithmetic and copies ran while one was open for 2% of the time, Pallas kernels for 0%

profile of v1, /device:TPU:0, one launch (start us, length us, event | category | flops | bytes accessed | tf_op | source)
XLA Modules:
  0.0 118.6 jit_solution(10593670190951121607)
XLA Ops:
  6.5 0.9 slice.63
  7.5 4.8 %collective-permute-start = (f32[128,1]{1,0:T(8,128)S(1)}, f32[128,1]{1,0:T(8,128)S(1)}, u32[]{:S(2)}, u32[]{:S(2)}) collective-permute-start(f32[128,1]{1,0:T(8,128)S(1)} %slice.63), channel_id=1, source_target_pairs={{0,2},{1,3},{4,6},{5,7},{8,10},{9,11},{12,14},{13,15},{16,18},{17,... | collective-permute-start | bytes 1544 | tf_op jit(solution)/shard_map/ppermute | solution.py:17
  12.3 0.7 divide_exponential_fusion
  13.0 1.2 %collective-permute-done = f32[128,1]{1,0:T(8,128)S(1)} collective-permute-done((f32[128,1]{1,0:T(8,128)S(1)}, f32[128,1]{1,0:T(8,128)S(1)}, u32[]{:S(2)}, u32[]{:S(2)}) %collective-permute-start) | collective-permute-done | bytes 544 | tf_op jit(solution)/shard_map/ppermute | solution.py:17
  14.2 1.4 %fusion.34 = f32[128,1024]{1,0:T(8,128)S(1)} fusion(f32[128,1024]{1,0:T(8,128)} %param.13, f32[128,1023]{1,0:T(8,128)} %bitcast.94, f32[128,1]{1,0:T(8,128)S(1)} %collective-permute-done, f32[128]{0:T(128)S(1)} %divide_exponential_fusion), kind=kLoop, calls=%fused_computation.55 | loop fusion | flops 393216 | bytes 1573376 | tf_op jit(solution)/shard_map/sub | solution.py:74
  15.7 3.5 %collective-permute-start.1 = (f32[64,1024]{1,0:T(8,128)S(1)}, f32[64,1024]{1,0:T(8,128)S(1)}, u32[]{:S(2)}, u32[]{:S(2)}) collective-permute-start(f32[64,1024]{1,0:T(8,128)S(1)} %get-tuple-element.238), channel_id=1, source_target_pairs={{0,4},{4,8},{8,12},{1,5},{5,9},{9,13},{2,6},{6,10},{10,14},{3,7},{... | collective-permute-start | bytes 786440 | tf_op jit(solution)/shard_map/ppermute | solution.py:25
  19.2 1.3 %collective-permute-start.2 = (f32[64,1024]{1,0:T(8,128)S(1)}, f32[64,1024]{1,0:T(8,128)S(1)}, u32[]{:S(2)}, u32[]{:S(2)}) collective-permute-start(f32[64,1024]{1,0:T(8,128)S(1)} %get-tuple-element.239), channel_id=1, source_target_pairs={{4,0},{8,4},{12,8},{5,1},{9,5},{13,9},{6,2},{10,6},{14,10},{7,3},{... | collective-permute-start | bytes 786440 | tf_op jit(solution)/shard_map/ppermute | solution.py:28
  20.5 3.4 %collective-permute-done.1 = f32[64,1024]{1,0:T(8,128)S(1)} collective-permute-done((f32[64,1024]{1,0:T(8,128)S(1)}, f32[64,1024]{1,0:T(8,128)S(1)}, u32[]{:S(2)}, u32[]{:S(2)}) %collective-permute-start.1) | collective-permute-done | bytes 262176 | tf_op jit(solution)/shard_map/ppermute | solution.py:25
  23.9 4.1 %collective-permute-done.2 = f32[64,1024]{1,0:T(8,128)S(1)} collective-permute-done((f32[64,1024]{1,0:T(8,128)S(1)}, f32[64,1024]{1,0:T(8,128)S(1)}, u32[]{:S(2)}, u32[]{:S(2)}) %collective-permute-start.2) | collective-permute-done | bytes 262176 | tf_op jit(solution)/shard_map/ppermute | solution.py:28
  28.1 0.8 fusion.25
  29.6 4.0 %collective-permute-start.3 = (f32[128,256]{1,0:T(8,128)S(1)}, f32[128,256]{1,0:T(8,128)S(1)}, u32[]{:S(2)}, u32[]{:S(2)}) collective-permute-start(f32[128,256]{1,0:T(8,128)S(1)} %get-tuple-element.236), channel_id=1, source_target_pairs={{0,2},{1,3},{4,6},{5,7},{8,10},{9,11},{12,14},{13,15},{16,18},{17,... | collective-permute-start | bytes 393224 | tf_op jit(solution)/shard_map/ppermute | solution.py:25
  33.6 1.3 %collective-permute-start.4 = (f32[128,256]{1,0:T(8,128)S(1)}, f32[128,256]{1,0:T(8,128)S(1)}, u32[]{:S(2)}, u32[]{:S(2)}) collective-permute-start(f32[128,256]{1,0:T(8,128)S(1)} %get-tuple-element.237), channel_id=1, source_target_pairs={{2,0},{3,1},{6,4},{7,5},{10,8},{11,9},{14,12},{15,13},{18,16},{19,... | collective-permute-start | bytes 393224 | tf_op jit(solution)/shard_map/ppermute | solution.py:28
  34.9 1.1 collective-permute-done.3
  36.0 4.4 %collective-permute-done.4 = f32[128,256]{1,0:T(8,128)S(1)} collective-permute-done((f32[128,256]{1,0:T(8,128)S(1)}, f32[128,256]{1,0:T(8,128)S(1)}, u32[]{:S(2)}, u32[]{:S(2)}) %collective-permute-start.4) | collective-permute-done | bytes 131104 | tf_op jit(solution)/shard_map/ppermute | solution.py:28
  42.1 13.0 %while.13 = (s32[]{:T(128)}, f32[2,128,2,128]{3,1,0,2:T(8,128)S(1)}, s32[2]{0:T(128)S(1)}, s32[]{:T(128)}, f32[128,1024]{1,0:T(8,128)S(1)}, /*index=5*/s32[]{:T(128)}, s32[]{:T(128)}, s32[1]{0:T(128)}) while((s32[]{:T(128)}, f32[2,128,2,128]{3,1,0,2:T(8,128)S(1)}, s32[2]{0:T(128)S(1)}, s32[]{:T(128)}, f32[128,1024]{1,0:T(8,128)S(1)}, ...), condition=%wide.region_5.6_spmd.clone, body=%wide.region_4.5_spmd.clone.sunk | while | flops 406373504 | bytes 1455749 | solution.py:104
  42.1 0.6 dynamic_slice.42
  43.4 2.6 %convolution_bitcast_fusion.2 = f32[128,1,128]{2,0,1:T(8,128)S(1)} fusion(f32[128,1024]{1,0:T(8,128)S(1)} %get-tuple-element.307, s32[1024]{0:T(1024)S(1)} %iota_add_fusion.6, s32[128]{0:T(128)S(1)} %iota_add_fusion.7), kind=kOutput, calls=%fused_computation.15.clone.1 | convolution fusion | flops 203161600 | bytes 594432 | tf_op jit(solution)/shard_map/while/body/eval_jaxpr/dot_general | solution.py:88
  46.0 2.6 %fusion.64 = f32[128,1,128]{2,0,1:T(8,128)S(1)} fusion(f32[128,1024]{1,0:T(8,128)S(1)} %get-tuple-element.307, s32[1024]{0:T(1024)S(1)} %iota_add_fusion.6, s32[128]{0:T(128)S(1)} %iota_add_fusion.7), kind=kOutput, calls=%fused_computation.14.clone.1 | convolution fusion | flops 203177984 | bytes 594432 | tf_op jit(solution)/shard_map/while/body/eval_jaxpr/dot_general | solution.py:95
  49.9 2.6 %convolution_bitcast_fusion.2 = f32[128,1,128]{2,0,1:T(8,128)S(1)} fusion(f32[128,1024]{1,0:T(8,128)S(1)} %get-tuple-element.307, s32[1024]{0:T(1024)S(1)} %iota_add_fusion.6, s32[128]{0:T(128)S(1)} %iota_add_fusion.7), kind=kOutput, calls=%fused_computation.15.clone.1 | convolution fusion | flops 203161600 | bytes 594432 | tf_op jit(solution)/shard_map/while/body/eval_jaxpr/dot_general | solution.py:88
  52.5 2.6 %fusion.64 = f32[128,1,128]{2,0,1:T(8,128)S(1)} fusion(f32[128,1024]{1,0:T(8,128)S(1)} %get-tuple-element.307, s32[1024]{0:T(1024)S(1)} %iota_add_fusion.6, s32[128]{0:T(128)S(1)} %iota_add_fusion.7), kind=kOutput, calls=%fused_computation.14.clone.1 | convolution fusion | flops 203177984 | bytes 594432 | tf_op jit(solution)/shard_map/while/body/eval_jaxpr/dot_general | solution.py:95
  55.1 0.7 copy-done.1
  55.9 0.7 fusion.43
  62.0 4.9 %reduce-scatter.3.cloned.1.call-done = f32[128,2,128]{2,0,1:T(8,128)} async-done(((f32[256,2,128]{2,0,1:T(8,128)}), f32[128,2,128]{2,0,1:T(8,128)}) %reduce-scatter.3.cloned.1.call-update) | async-done | bytes 131088 | tf_op jit(solution)/shard_map/reduce_scatter | solution.py:105
  66.9 1.0 multiply_reduce_fusion
  67.9 5.8 %psum.7 = f32[128]{0:T(128)S(1)} all-reduce(f32[128]{0:T(128)S(1)} %multiply_reduce_fusion), channel_id=1, replica_groups=mesh['groups'=2,'chan'=4,'tm'=2,'band'=2] {'tm','band'}, use_global_device_ids=true, to_apply=%region_8.9 | all-reduce | flops 128 | bytes 1024 | tf_op jit(solution)/shard_map/psum | solution.py:112
  73.7 0.9 fusion.40
  74.6 1.7 %collective-permute-start.5 = (bf16[128,2,128]{2,0,1:T(8,128)(2,1)S(1)}, bf16[128,2,128]{2,0,1:T(8,128)(2,1)S(1)}, u32[]{:S(2)}, u32[]{:S(2)}) collective-permute-start(bf16[128,2,128]{2,0,1:T(8,128)(2,1)S(1)} %get-tuple-element.235), channel_id=1, source_target_pairs={{0,4},{4,8},{8,12},{12,0},{1,5},{5,9},{9,13},{13,1},{2,6},{6,10},{... | collective-permute-start | bytes 196616 | tf_op jit(solution)/shard_map/ppermute | solution.py:151
  76.3 2.2 %collective-permute-start.6 = (bf16[128,2,128]{2,0,1:T(8,128)(2,1)S(1)}, bf16[128,2,128]{2,0,1:T(8,128)(2,1)S(1)}, u32[]{:S(2)}, u32[]{:S(2)}) collective-permute-start(bf16[128,2,128]{2,0,1:T(8,128)(2,1)S(1)} %get-tuple-element.235), channel_id=1, source_target_pairs={{0,12},{4,0},{8,4},{12,8},{1,13},{5,1},{9,5},{13,9},{2,14},{6,2},{... | collective-permute-start | bytes 196616 | tf_op jit(solution)/shard_map/ppermute | solution.py:156
  79.3 2.0 %collective-permute-done.5 = bf16[128,2,128]{2,0,1:T(8,128)(2,1)S(1)} collective-permute-done((bf16[128,2,128]{2,0,1:T(8,128)(2,1)S(1)}, bf16[128,2,128]{2,0,1:T(8,128)(2,1)S(1)}, u32[]{:S(2)}, u32[]{:S(2)}) %collective-permute-start.5) | collective-permute-done | bytes 65568 | tf_op jit(solution)/shard_map/ppermute | solution.py:151
  81.6 5.8 %collective-permute-done.7 = bf16[128,2,128]{2,0,1:T(8,128)(2,1)S(1)} collective-permute-done((bf16[128,2,128]{2,0,1:T(8,128)(2,1)S(1)}, bf16[128,2,128]{2,0,1:T(8,128)(2,1)S(1)}, u32[]{:S(2)}, u32[]{:S(2)}) %collective-permute-start.7) | collective-permute-done | bytes 65568 | tf_op jit(solution)/shard_map/ppermute | solution.py:151
  89.6 0.9 pad_maximum_fusion.1
  90.6 21.2 %reduce-scatter.5.cloned.1.call-done = f32[1,4,3,32,128]{4,3,2,1,0:T(8,128)} async-done(((f32[1,4,3,128,128]{4,3,2,1,0:T(8,128)}), f32[1,4,3,32,128]{4,3,2,1,0:T(8,128)}) %reduce-scatter.5.cloned.1.call-update) | async-done | bytes 196624 | tf_op jit(solution)/shard_map/reduce_scatter | solution.py:183
  (70 shorter events, 8.7 us)
Async XLA Ops:
  6.5 28.4 %copy-start = (s32[4,4]{1,0:T(4,128)S(1)}, s32[4,4]{1,0:T(4,128)}, u32[]{:S(2)}) copy-start(s32[4,4]{1,0:T(4,128)} %param.15) | copy-start | bytes 196
  6.5 60.4 %reduce-scatter.3.cloned.1.call-start = ((), (), s32[]{:S(2)}) async-start(), calls=%async_computation.2 | async-start | bytes 393216 | tf_op jit(solution)/shard_map/reduce_scatter | solution.py:105
  7.5 6.7 %collective-permute-start = (f32[128,1]{1,0:T(8,128)S(1)}, f32[128,1]{1,0:T(8,128)S(1)}, u32[]{:S(2)}, u32[]{:S(2)}) collective-permute-start(f32[128,1]{1,0:T(8,128)S(1)} %slice.63), channel_id=1, source_target_pairs={{0,2},{1,3},{4,6},{5,7},{8,10},{9,11},{12,14},{13,15},{16,18},{17,... | collective-permute-start | bytes 1544 | tf_op jit(solution)/shard_map/ppermute | solution.py:17
  15.7 8.2 %collective-permute-start.1 = (f32[64,1024]{1,0:T(8,128)S(1)}, f32[64,1024]{1,0:T(8,128)S(1)}, u32[]{:S(2)}, u32[]{:S(2)}) collective-permute-start(f32[64,1024]{1,0:T(8,128)S(1)} %get-tuple-element.238), channel_id=1, source_target_pairs={{0,4},{4,8},{8,12},{1,5},{5,9},{9,13},{2,6},{6,10},{10,14},{3,7},{... | collective-permute-start | bytes 786440 | tf_op jit(solution)/shard_map/ppermute | solution.py:25
  19.2 8.8 %collective-permute-start.2 = (f32[64,1024]{1,0:T(8,128)S(1)}, f32[64,1024]{1,0:T(8,128)S(1)}, u32[]{:S(2)}, u32[]{:S(2)}) collective-permute-start(f32[64,1024]{1,0:T(8,128)S(1)} %get-tuple-element.239), channel_id=1, source_target_pairs={{4,0},{8,4},{12,8},{5,1},{9,5},{13,9},{6,2},{10,6},{14,10},{7,3},{... | collective-permute-start | bytes 786440 | tf_op jit(solution)/shard_map/ppermute | solution.py:28
  29.6 6.5 %collective-permute-start.3 = (f32[128,256]{1,0:T(8,128)S(1)}, f32[128,256]{1,0:T(8,128)S(1)}, u32[]{:S(2)}, u32[]{:S(2)}) collective-permute-start(f32[128,256]{1,0:T(8,128)S(1)} %get-tuple-element.236), channel_id=1, source_target_pairs={{0,2},{1,3},{4,6},{5,7},{8,10},{9,11},{12,14},{13,15},{16,18},{17,... | collective-permute-start | bytes 393224 | tf_op jit(solution)/shard_map/ppermute | solution.py:25
  33.6 6.9 %collective-permute-start.4 = (f32[128,256]{1,0:T(8,128)S(1)}, f32[128,256]{1,0:T(8,128)S(1)}, u32[]{:S(2)}, u32[]{:S(2)}) collective-permute-start(f32[128,256]{1,0:T(8,128)S(1)} %get-tuple-element.237), channel_id=1, source_target_pairs={{2,0},{3,1},{6,4},{7,5},{10,8},{11,9},{14,12},{15,13},{18,16},{19,... | collective-permute-start | bytes 393224 | tf_op jit(solution)/shard_map/ppermute | solution.py:28
  55.1 0.7 copy-start.1
  55.8 55.9 %reduce-scatter.5.cloned.1.call-start = ((), (), s32[]{:S(2)}) async-start(), calls=%async_computation.3 | async-start | bytes 983040 | tf_op jit(solution)/shard_map/reduce_scatter | solution.py:183
  74.6 6.8 %collective-permute-start.5 = (bf16[128,2,128]{2,0,1:T(8,128)(2,1)S(1)}, bf16[128,2,128]{2,0,1:T(8,128)(2,1)S(1)}, u32[]{:S(2)}, u32[]{:S(2)}) collective-permute-start(bf16[128,2,128]{2,0,1:T(8,128)(2,1)S(1)} %get-tuple-element.235), channel_id=1, source_target_pairs={{0,4},{4,8},{8,12},{12,0},{1,5},{5,9},{9,13},{13,1},{2,6},{6,10},{... | collective-permute-start | bytes 196616 | tf_op jit(solution)/shard_map/ppermute | solution.py:151
  76.3 5.2 %collective-permute-start.6 = (bf16[128,2,128]{2,0,1:T(8,128)(2,1)S(1)}, bf16[128,2,128]{2,0,1:T(8,128)(2,1)S(1)}, u32[]{:S(2)}, u32[]{:S(2)}) collective-permute-start(bf16[128,2,128]{2,0,1:T(8,128)(2,1)S(1)} %get-tuple-element.235), channel_id=1, source_target_pairs={{0,12},{4,0},{8,4},{12,8},{1,13},{5,1},{9,5},{13,9},{2,14},{6,2},{... | collective-permute-start | bytes 196616 | tf_op jit(solution)/shard_map/ppermute | solution.py:156
  81.4 6.1 %collective-permute-start.7 = (bf16[128,2,128]{2,0,1:T(8,128)(2,1)S(1)}, bf16[128,2,128]{2,0,1:T(8,128)(2,1)S(1)}, u32[]{:S(2)}, u32[]{:S(2)}) collective-permute-start(bf16[128,2,128]{2,0,1:T(8,128)(2,1)S(1)} %collective-permute-done.5), channel_id=1, source_target_pairs={{0,4},{4,8},{8,12},{12,0},{1,5},{5,9},{9,13},{13,1},{2,6},{6,10},{... | collective-permute-start | bytes 196616 | tf_op jit(solution)/shard_map/ppermute | solution.py:151
Sparse Core Ops, SparseCore 0:
  56.0 10.9 reduce-scatter.2
  90.7 20.9 reduce-scatter.4
